TPU v7x, 512 devices: a whole 4x4x16 slice. The times are simulated.
512 devices in a mesh: group: 64 (over x, z_lo, core), tensor: 8 (over y, z_hi).
Axes of the slice: x: 4, y: 4, z: 16 (z_hi: 2, z_lo: 8; z = z_hi * 8 + z_lo), core: 2. Of those that a mesh axis runs over, the one named last changes fastest.
Arguments:
- cache_blocks: bfloat16 [4096, 1, 128, 8, 256], P('group', None, 'tensor'), may hold values from -6 to 6
- prompt_len: int32 [64, 64], replicated, may hold values from 1 to 128, 2730 in all within a row
- dest_perm: int32 [64, 64], replicated, may hold values from 0 to 63, each once within a row
- new_q: bfloat16 [64, 64, 4, 64, 128], P('group', None, None, 'tensor'), may hold values from -170 to 170
- new_kv: bfloat16 [64, 64, 4, 8, 256], P('group', None, None, 'tensor'), may hold values from -6 to 6
Outputs:
- attended: bfloat16 [64, 64, 4, 64, 128], P('group', None, None, 'tensor')
Inputs may be any that keep to these rules, and one draw needn't show every extreme that they name: Prompt j of group s goes to decode group dest_perm[s, j]; each row of dest_perm names every decode group once, so every decode group receives exactly one prompt from each holding group. `prompt_len`: the lengths of one group's prompts sum to 2730, and one of them is 128.
All inputs are finite; a program needn't handle non-finite values.
Results may differ from a plain program's by a relative error of at most 0.0049.
Values may be sent and summed in bfloat16 or wider, within the bound.
A program may use at most 64 MiB of HBM per device.

v0:
```python
import math

import jax
import jax.numpy as jnp
from jax import lax
from jax.sharding import PartitionSpec as P


def shards(cache_blocks, prompt_len, dest_perm, new_q, new_kv):
    groups = lax.axis_size("group")
    own_group = lax.axis_index("group")
    requests = cache_blocks.shape[0]
    group_ids = jnp.arange(groups, dtype=jnp.int32)
    own_order = lax.dynamic_index_in_dim(dest_perm, own_group, 0, keepdims=False)
    send_match = own_order[:, None] == group_ids[None, :]
    send_position = jnp.sum(jnp.where(send_match, group_ids[:, None], 0), axis=0)
    send_live = send_position < requests
    send_index = jnp.minimum(send_position, requests - 1)
    by_head = lax.all_to_all(cache_blocks, "tensor", split_axis=3, concat_axis=2, tiled=True)
    chosen = jnp.take(by_head, send_index, axis=0)
    received = lax.all_to_all(
        jnp.where(send_live[:, None, None, None, None], chosen, jnp.zeros_like(chosen)),
        "group",
        split_axis=0,
        concat_axis=0,
        tiled=True,
    )
    recv_match = dest_perm == own_group
    recv_position = jnp.sum(jnp.where(recv_match, group_ids[None, :], 0), axis=1)
    recv_live = recv_position < requests
    recv_index = jnp.minimum(recv_position, requests - 1)
    context_len = jnp.where(
        recv_live, jnp.take_along_axis(prompt_len, recv_index[:, None], axis=1)[:, 0], 0
    )
    slots, blocks, width, heads_here, paired = received.shape
    head_dim = paired // 2
    context = received.reshape(slots, blocks * width, heads_here, paired)
    ctx_keys = context[..., :head_dim]
    ctx_vals = context[..., head_dim:]
    step_count = new_q.shape[2]
    q_here = new_q.shape[3]
    share = q_here // heads_here
    queries = new_q[0].reshape(slots, step_count, heads_here, share, head_dim)
    fresh = new_kv[0]
    fresh_keys = fresh[..., :head_dim]
    fresh_vals = fresh[..., head_dim:]
    score_scale = 1.0 / math.sqrt(head_dim)
    ctx_scores = (
        jnp.einsum("stkgd,spkd->stkgp", queries, ctx_keys, preferred_element_type=jnp.float32)
        * score_scale
    )
    new_scores = (
        jnp.einsum("stkgd,sukd->stkgu", queries, fresh_keys, preferred_element_type=jnp.float32)
        * score_scale
    )
    token_pos = jnp.arange(blocks * width, dtype=jnp.int32)
    ctx_mask = token_pos[None, :] < context_len[:, None]
    ctx_scores = jnp.where(ctx_mask[:, None, None, None, :], ctx_scores, -1e30)
    step_ids = jnp.arange(step_count, dtype=jnp.int32)
    causal = step_ids[None, :] <= step_ids[:, None]
    new_scores = jnp.where(causal[None, :, None, None, :], new_scores, -1e30)
    row_max = jnp.maximum(jnp.max(ctx_scores, axis=-1), jnp.max(new_scores, axis=-1))
    ctx_expo = jnp.exp(ctx_scores - row_max[..., None])
    new_expo = jnp.exp(new_scores - row_max[..., None])
    denominator = jnp.sum(ctx_expo, axis=-1) + jnp.sum(new_expo, axis=-1)
    ctx_probs = (ctx_expo / denominator[..., None]).astype(jnp.bfloat16)
    new_probs = (new_expo / denominator[..., None]).astype(jnp.bfloat16)
    result = jnp.einsum(
        "stkgp,spkd->stkgd", ctx_probs, ctx_vals, preferred_element_type=jnp.float32
    )
    result = result + jnp.einsum(
        "stkgu,sukd->stkgd", new_probs, fresh_vals, preferred_element_type=jnp.float32
    )
    return result.reshape(1, slots, step_count, q_here, head_dim).astype(jnp.bfloat16)


def solution(mesh):
    placed = (
        P("group", None, "tensor", None, None),
        P(),
        P(),
        P("group", None, None, "tensor", None),
        P("group", None, None, "tensor", None),
    )
    return jax.shard_map(
        shards,
        mesh=mesh,
        in_specs=placed,
        out_specs=P("group", None, None, "tensor", None),
        check_vma=False,
    )
```

profile of v0, /device:TPU:1, one launch (start us, length us, event | category | flops | bytes accessed | tf_op | source)
XLA Modules:
  0.0 432.8 jit_solution(17980820110161655050)
XLA Ops:
  0.0 0.0 copy-start
  0.0 5.1 %copy.7 = bf16[64,1,16,8,256]{4,2,0,1,3:T(8,128)(2,1)} copy(bf16[64,1,16,8,256]{4,3,2,1,0:T(8,128)(2,1)} %param.5) | data formatting | bytes 8388608 | tf_op args[0]
  5.1 0.0 copy-start.2
  5.1 18.4 %all-to-all-start = ((bf16[64,1,16,8,256]{4,2,0,1,3:T(8,128)(2,1)}), bf16[64,1,16,8,256]{4,2,0,1,3:T(8,128)(2,1)}, u32[]{:S(2)}, u32[]{:S(2)}) async-start(bf16[64,1,16,8,256]{4,2,0,1,3:T(8,128)(2,1)} %copy.7), calls=%async_computation | async-start | bytes 8388608 | tf_op jit(solution)/shard_map/all_to_all | solution.py:19
  23.5 0.0 copy-done.2
  23.5 0.1 select_reduce_fusion.1
  23.6 91.9 %all-to-all-done = bf16[64,1,16,8,256]{4,2,0,1,3:T(8,128)(2,1)} async-done(((bf16[64,1,16,8,256]{4,2,0,1,3:T(8,128)(2,1)}), bf16[64,1,16,8,256]{4,2,0,1,3:T(8,128)(2,1)}, u32[]{:S(2)}, u32[]{:S(2)}) %all-to-all-start) | async-done | bytes 4194336 | tf_op jit(solution)/shard_map/all_to_all | solution.py:19
  115.6 4.8 %copy.8 = bf16[64,1,16,8,256]{4,2,3,0,1:T(8,128)(2,1)} copy(bf16[64,1,16,8,256]{4,2,0,1,3:T(8,128)(2,1)} %all-to-all-done) | data formatting | bytes 8388608 | tf_op jit(solution)/shard_map/all_to_all | solution.py:19
  120.4 4.9 %gather_fusion = bf16[64,128,256]{2,1,0:T(8,128)(2,1)} fusion(bf16[64,128,256]{2,1,0:T(8,128)(2,1)} %bitcast.106, s32[1024]{0:T(1024)S(1)} %pad_clamp_fusion), kind=kCustom, calls=%fused_computation | custom fusion | bytes 8388864 | tf_op jit(solution)/shard_map/jit(_take)/gather | solution.py:20
  125.3 3.9 fusion.1
  129.2 0.0 copy-start.1
  129.2 0.0 copy-start.3
  129.2 110.0 %all-to-all-start.1 = ((bf16[64,1,128,1,256]{4,2,3,1,0:T(8,128)(2,1)}), bf16[64,1,128,1,256]{4,2,3,1,0:T(8,128)(2,1)}, u32[]{:S(2)}, u32[]{:S(2)}) async-start(bf16[64,1,128,1,256]{4,2,3,1,0:T(8,128)(2,1)} %fusion.1), calls=%async_computation.1 | async-start | bytes 8388608 | tf_op jit(solution)/shard_map/all_to_all | solution.py:21
  239.2 0.1 select_reduce_fusion
  239.4 0.0 copy-done.1
  239.4 0.8 gather_fusion.1
  240.2 0.1 iota_compare_fusion
  240.3 0.0 copy-done
  240.3 0.0 copy-done.3
  240.3 2.4 fusion.23
  242.8 182.3 %all-to-all-done.1 = bf16[64,1,128,1,256]{4,2,3,1,0:T(8,128)(2,1)} async-done(((bf16[64,1,128,1,256]{4,2,3,1,0:T(8,128)(2,1)}), bf16[64,1,128,1,256]{4,2,3,1,0:T(8,128)(2,1)}, u32[]{:S(2)}, u32[]{:S(2)}) %all-to-all-start.1) | async-done | bytes 4194336 | tf_op jit(solution)/shard_map/all_to_all | solution.py:21
  425.1 2.9 fusion.22
  428.0 0.7 fusion.13
  428.8 0.5 fusion.18
  429.3 2.2 fusion.3
  431.5 1.3 fusion.10
  (12 shorter events, 0.2 us)
Async XLA Ops:
  0.0 240.3 %copy-start = (bf16[1,64,4,8,128]{4,3,2,1,0:T(8,128)(2,1)S(1)}, bf16[1,64,4,8,128]{4,3,2,1,0:T(8,128)(2,1)}, u32[]{:S(2)}) copy-start(bf16[1,64,4,8,128]{4,3,2,1,0:T(8,128)(2,1)} %param.8) | copy-start | bytes 1572868
  5.1 18.4 %copy-start.2 = (s32[64,64]{1,0:T(8,128)S(1)}, s32[64,64]{1,0:T(8,128)}, u32[]{:S(2)}) copy-start(s32[64,64]{1,0:T(8,128)} %param.7) | copy-start | bytes 49156
  5.1 110.5 %all-to-all-start = ((bf16[64,1,16,8,256]{4,2,0,1,3:T(8,128)(2,1)}), bf16[64,1,16,8,256]{4,2,0,1,3:T(8,128)(2,1)}, u32[]{:S(2)}, u32[]{:S(2)}) async-start(bf16[64,1,16,8,256]{4,2,0,1,3:T(8,128)(2,1)} %copy.7), calls=%async_computation | async-start | bytes 8388608 | tf_op jit(solution)/shard_map/all_to_all | solution.py:19
  129.2 110.2 %copy-start.1 = (s32[64,64]{1,0:T(8,128)S(1)}, s32[64,64]{1,0:T(8,128)}, u32[]{:S(2)}) copy-start(s32[64,64]{1,0:T(8,128)} %param.6) | copy-start | bytes 49156
  129.2 111.1 %copy-start.3 = (bf16[1,64,4,1,256]{4,2,3,1,0:T(4,128)(2,1)S(1)}, bf16[1,64,4,1,256]{4,2,3,1,0:T(4,128)(2,1)}, u32[]{:S(2)}) copy-start(bf16[1,64,4,1,256]{4,2,3,1,0:T(4,128)(2,1)} %param.9) | copy-start | bytes 393220
  129.2 295.9 %all-to-all-start.1 = ((bf16[64,1,128,1,256]{4,2,3,1,0:T(8,128)(2,1)}), bf16[64,1,128,1,256]{4,2,3,1,0:T(8,128)(2,1)}, u32[]{:S(2)}, u32[]{:S(2)}) async-start(bf16[64,1,128,1,256]{4,2,3,1,0:T(8,128)(2,1)} %fusion.1), calls=%async_computation.1 | async-start | bytes 8388608 | tf_op jit(solution)/shard_map/all_to_all | solution.py:21
where the time goes:
time: 434 us; the launch traced here: 433 us
  waiting for transfers between devices  274 us (63%)
  starting transfers between devices  128 us (29%)
  local copies, waits for them, and re-layouts  15.6 us (4%)
  matrix products  8.83 us (2%)
  other arithmetic  5.58 us (1%)
    all_to_all x1, waiting for transfers between devices, shards(): lax.all_to_all(jnp.where(send_live[:, None, None, None, None], chosen, jn...  182 us
    all_to_all x1, starting transfers between devices, shards(): lax.all_to_all(jnp.where(send_live[:, None, None, None, None], chosen, jn...  110 us
    all_to_all x1, waiting for transfers between devices, shards(): lax.all_to_all(cache_blocks, 'tensor', split_axis=3, concat_axis=2, tiled...  91.9 us
    all_to_all x1, starting transfers between devices, shards(): lax.all_to_all(cache_blocks, 'tensor', split_axis=3, concat_axis=2, tiled...  18.4 us
  transfers between devices with their start and end apart: 2, of which 2 were waited for; matrix products, arithmetic and copies ran while one was open for 1% of the time, Pallas kernels for 0%

commit v1 on v0

v1 whole, which is shorter than its diff:
```python
import functools
import math

import jax
import jax.numpy as jnp
from jax import lax
from jax.experimental import pallas as pl
from jax.experimental.pallas import tpu as pltpu
from jax.sharding import PartitionSpec as P

MESH = pl.DeviceIdType.MESH

X, ZL, CORES = 4, 8, 2
ZH = 2
CHUNKS = 8
NONE = -1e30


def kernel(groups, tensors, cache_ref, pos_ref, len_ref, q_ref, fresh_ref, out_ref,
           cbuf, kvsend, kvrecv, qbuf, osend, orecv, ssend, srecv, fo, fm, fl,
           cache_sem, kv_send_sem, kv_recv_sem, q_send_sem, q_recv_sem,
           o_send_sem, o_recv_sem, s_send_sem, s_recv_sem):
    ys = tensors // ZH
    g = lax.axis_index("group")
    t = lax.axis_index("tensor")
    y, zh = t // ZH, t % ZH
    core, zl, x = g % CORES, (g // CORES) % ZL, g // (CORES * ZL)
    z = zh * ZL + zl
    rows = q_ref.shape[0]
    qn = q_ref.shape[1]
    head = q_ref.shape[2]
    tok = cache_ref.shape[1] // tensors
    piece = ZH * tok
    per = rows // CHUNKS
    scale = 1.0 / math.sqrt(head)
    inner = X * CORES

    def offsets(i):
        k, j = i // inner, inner - 1 - i % inner
        far = ZL // 2 + (k // 2) * (1 - k % 2) - ((k + 1) // 2) * (k % 2)
        return j // CORES, far, j % CORES

    def towards(i):
        dx, dz, dc = offsets(i)
        peer = (((x + dx) % X) * ZL + (zl + dz) % ZL) * CORES + (core + dc) % CORES
        return peer

    def source(i):
        dx, dz, dc = offsets(i)
        return (((x + X - dx) % X) * ZL + (zl + ZL - dz) % ZL) * CORES + (core + CORES - dc) % CORES

    last = groups - 1

    def cache_copy(c):
        return pltpu.make_async_copy(
            cache_ref.at[pl.ds(c * per, per)], cbuf.at[pl.ds(c * per, per)], cache_sem.at[c])

    for c in range(CHUNKS):
        cache_copy(c).start()

    barrier = pltpu.get_barrier_semaphore()

    def greet(i, _):
        peer = towards(i)
        for h in range(ZH):
            pl.semaphore_signal(barrier, inc=1, device_id=(peer, y * ZH + h), device_id_type=MESH)
        return 0

    lax.fori_loop(0, last, greet, 0)
    pl.semaphore_signal(barrier, inc=1, device_id=(g, y * ZH + 1 - zh), device_id_type=MESH)
    for k in range(1, ys):
        pl.semaphore_signal(barrier, inc=1, device_id=(g, ((y + k) % ys) * ZH + zh), device_id_type=MESH)
    pl.semaphore_wait(barrier, groups * ZH - 1 + ys - 1)

    def q_copy(peer, h):
        return pltpu.make_async_remote_copy(
            src_ref=q_ref.at[peer], dst_ref=qbuf.at[g, zh], send_sem=q_send_sem,
            recv_sem=q_recv_sem.at[g], device_id=(peer, y * ZH + h), device_id_type=MESH)

    def send_q(i, _):
        peer = towards(i)
        for h in range(ZH):
            q_copy(peer, h).start()
        return 0

    lax.fori_loop(0, last, send_q, 0)
    q_copy(g, 1 - zh).start()
    pltpu.make_async_copy(q_ref.at[g], qbuf.at[g, zh], q_recv_sem.at[g]).start()

    size = tensors * tok
    r_out = lax.broadcasted_iota(jnp.int32, (size, size), 0)
    r_in = lax.broadcasted_iota(jnp.int32, (size, size), 1)
    pair = r_out // piece + y
    pair = jnp.where(pair >= ys, pair - ys, pair)
    wanted = (r_out % tok) * tensors + pair * ZH + (r_out % piece) // tok
    shuffle = jnp.where(wanted == r_in, 1.0, 0.0).astype(jnp.bfloat16)

    def kv_copy(k, c):
        return pltpu.make_async_remote_copy(
            src_ref=kvsend.at[k - 1, pl.ds(c * per, per)],
            dst_ref=kvrecv.at[pl.ds(c * per, per), y],
            send_sem=kv_send_sem.at[k - 1, c], recv_sem=kv_recv_sem.at[k - 1, c],
            device_id=(g, ((y + k) % ys) * ZH + zh), device_id_type=MESH)

    for c in range(CHUNKS):
        cache_copy(c).wait()

        def regroup(i, _, c=c):
            r = c * per + i
            moved = jnp.dot(shuffle, cbuf[r], preferred_element_type=jnp.float32).astype(jnp.bfloat16)
            kvrecv[r, y] = moved[:piece]
            for k in range(1, ys):
                kvsend[k - 1, r] = moved[k * piece:(k + 1) * piece]
            return 0

        lax.fori_loop(0, per, regroup, 0)
        for k in range(1, ys):
            kv_copy(k, c).start()

    batch, fresh_rows = fresh_ref.shape[0], fresh_ref.shape[1]
    at = rows // batch
    steps = fresh_rows // at
    shape = (at * qn, fresh_rows)
    f_row = lax.broadcasted_iota(jnp.int32, shape, 0)
    f_col = lax.broadcasted_iota(jnp.int32, shape, 1)
    f_keep = ((f_row // qn) == (f_col // steps)) & ((f_col % steps) <= (f_row % qn) // (qn // steps))

    def fresh_part(b, _):
        q = q_ref[pl.ds(b * at, at)].reshape(at * qn, head)
        kv = fresh_ref[b]
        s = lax.dot_general(q, kv[:, :head], (((1,), (1,)), ((), ())), preferred_element_type=jnp.float32) * scale
        s = jnp.where(f_keep, s, NONE)
        m = jnp.max(s, axis=1, keepdims=True)
        p = jnp.exp(s - m)
        l = jnp.sum(p, axis=1, keepdims=True)
        o = jnp.dot(p.astype(jnp.bfloat16), kv[:, head:], preferred_element_type=jnp.float32)
        fo[pl.ds(b * at, at)] = o.reshape(at, qn, head)
        fm[pl.ds(b * at, at)] = jnp.broadcast_to(m, (at * qn, head)).reshape(at, qn, head)
        fl[pl.ds(b * at, at)] = jnp.broadcast_to(l, (at * qn, head)).reshape(at, qn, head)
        return 0

    lax.fori_loop(0, batch, fresh_part, 0)

    for c in range(CHUNKS):
        for k in range(1, ys):
            kv_copy(k, c).wait_recv()

    both = ZH * qn
    shape = (both, ys * piece)
    a_row = lax.broadcasted_iota(jnp.int32, shape, 0)
    a_col = lax.broadcasted_iota(jnp.int32, shape, 1)
    token = ((a_col // piece) * ZH + zh) * tok + a_col % tok
    token = jnp.where((a_col % piece) // tok == a_row // qn, token, 1 << 20)
    lane = lax.broadcasted_iota(jnp.int32, (both, head), 1)
    diag = lax.broadcasted_iota(jnp.int32, (both, head), 0) % qn
    on_m, on_l = lane == diag, lane == diag + qn

    def o_copy(peer, h):
        return pltpu.make_async_remote_copy(
            src_ref=osend.at[peer, h], dst_ref=orecv.at[g, zh], send_sem=o_send_sem,
            recv_sem=o_recv_sem.at[g], device_id=(peer, y * ZH + h), device_id_type=MESH)

    def s_copy(peer, h):
        return pltpu.make_async_remote_copy(
            src_ref=ssend.at[peer, h], dst_ref=srecv.at[g, zh], send_sem=s_send_sem,
            recv_sem=s_recv_sem.at[g], device_id=(peer, y * ZH + h), device_id_type=MESH)

    def attend(i):
        src = source(i)
        pltpu.make_async_copy(qbuf.at[src], qbuf.at[src], q_recv_sem.at[src]).wait()
        q = qbuf[src].reshape(both, head)
        kv = kvrecv[pos_ref[src]].reshape(ys * piece, 2 * head)
        s = lax.dot_general(q, kv[:, :head], (((1,), (1,)), ((), ())), preferred_element_type=jnp.float32) * scale
        keep = token < len_ref[src]
        s = jnp.where(keep, s, NONE)
        m = jnp.max(s, axis=1, keepdims=True)
        p = jnp.where(keep, jnp.exp(s - m), 0.0)
        l = jnp.sum(p, axis=1, keepdims=True)
        o = jnp.dot(p.astype(jnp.bfloat16), kv[:, head:], preferred_element_type=jnp.float32)
        osend[src] = o.astype(jnp.bfloat16).reshape(ZH, qn, head)
        stat = jnp.where(on_m, m, jnp.where(on_l, l, 0.0))
        ssend[src] = jnp.sum(stat.reshape(ZH, qn, head), axis=1, keepdims=True)
        return src

    def attend_send(i, _):
        src = attend(i)
        for h in range(ZH):
            o_copy(src, h).start()
            s_copy(src, h).start()
        return 0

    lax.fori_loop(0, last, attend_send, 0)
    attend(last)
    o_copy(g, 1 - zh).start()
    s_copy(g, 1 - zh).start()
    pltpu.make_async_copy(osend.at[g, zh], orecv.at[g, zh], o_recv_sem.at[g]).start()
    pltpu.make_async_copy(ssend.at[g, zh], srecv.at[g, zh], s_recv_sem.at[g]).start()

    c_lane = lax.broadcasted_iota(jnp.int32, (qn, head), 1)
    c_row = lax.broadcasted_iota(jnp.int32, (qn, head), 0)

    def combine(i, _):
        src = towards(i)
        pltpu.make_async_copy(orecv.at[src], orecv.at[src], o_recv_sem.at[src]).wait()
        pltpu.make_async_copy(srecv.at[src], srecv.at[src], s_recv_sem.at[src]).wait()
        m, l, o = [fm[src]], [fl[src]], [fo[src]]
        for h in range(ZH):
            stat = jnp.broadcast_to(srecv[src, h], (qn, head))
            m.append(jnp.sum(jnp.where(c_lane == c_row, stat, 0.0), axis=1, keepdims=True))
            l.append(jnp.sum(jnp.where(c_lane == c_row + qn, stat, 0.0), axis=1, keepdims=True))
            o.append(orecv[src, h].astype(jnp.float32))
        top = functools.reduce(jnp.maximum, m)
        w = [jnp.exp(a - top) for a in m]
        den = sum(a * b for a, b in zip(w, l))
        num = sum(a * b for a, b in zip(w, o))
        out_ref[src] = (num / den).astype(jnp.bfloat16)
        return 0

    lax.fori_loop(0, groups, combine, 0)

    for c in range(CHUNKS):
        for k in range(1, ys):
            kv_copy(k, c).wait_send()
    for ref, sem in ((qbuf, q_send_sem), (osend, o_send_sem), (ssend, s_send_sem)):
        pltpu.make_async_copy(ref.at[pl.ds(0, last)], ref.at[pl.ds(0, last)], sem).wait()
        pltpu.make_async_copy(ref.at[last, 0], ref.at[last, 0], sem).wait()


def shards(cache_blocks, prompt_len, dest_perm, new_q, new_kv):
    groups = lax.axis_size("group")
    tensors = lax.axis_size("tensor")
    own = lax.axis_index("group")
    requests, _, tok, heads, width = cache_blocks.shape
    head = width // 2
    slots, steps, q_here = new_q.shape[1:4]
    qn = steps * q_here
    ids = jnp.arange(groups, dtype=jnp.int32)
    order = lax.dynamic_index_in_dim(dest_perm, own, 0, keepdims=False)
    lens = lax.dynamic_index_in_dim(prompt_len, own, 0, keepdims=False)
    match = order[:, None] == ids[None, :]
    position = jnp.sum(jnp.where(match, ids[:, None], 0), axis=0)
    length = jnp.sum(jnp.where(match, lens[:, None], 0), axis=0)
    cache = cache_blocks.reshape(requests, tok * heads, width)
    queries = new_q.reshape(slots, qn, head)
    fresh = new_kv.reshape(CHUNKS, slots // CHUNKS * steps, width)
    ys = tensors // ZH
    piece = ZH * tok
    bf16, f32 = jnp.bfloat16, jnp.float32
    vmem = pl.BlockSpec(memory_space=pltpu.VMEM)
    smem = pl.BlockSpec(memory_space=pltpu.SMEM)
    dma = pltpu.SemaphoreType.DMA
    out = pl.pallas_call(
        functools.partial(kernel, groups, tensors),
        out_shape=jax.ShapeDtypeStruct((slots, qn, head), bf16),
        in_specs=[pl.BlockSpec(memory_space=pl.ANY), smem, smem, vmem, vmem],
        out_specs=vmem,
        scratch_shapes=[
            pltpu.VMEM((requests, tok * heads, width), bf16),
            pltpu.VMEM((ys - 1, requests, piece, width), bf16),
            pltpu.VMEM((requests, ys, piece, width), bf16),
            pltpu.VMEM((groups, ZH, qn, head), bf16),
            pltpu.VMEM((groups, ZH, qn, head), bf16),
            pltpu.VMEM((groups, ZH, qn, head), bf16),
            pltpu.VMEM((groups, ZH, 1, head), f32),
            pltpu.VMEM((groups, ZH, 1, head), f32),
            pltpu.VMEM((slots, qn, head), f32),
            pltpu.VMEM((slots, qn, head), f32),
            pltpu.VMEM((slots, qn, head), f32),
            dma((CHUNKS,)),
            dma((ys - 1, CHUNKS)),
            dma((ys - 1, CHUNKS)),
            dma,
            dma((groups,)),
            dma,
            dma((groups,)),
            dma,
            dma((groups,)),
        ],
        compiler_params=pltpu.CompilerParams(
            collective_id=0, has_side_effects=True, vmem_limit_bytes=48 << 20),
        cost_estimate=pl.CostEstimate(flops=1 << 30, bytes_accessed=12 << 20, transcendentals=1 << 20),
    )(cache, position, length, queries, fresh)
    return out.reshape(1, slots, steps, q_here, head)


def solution(mesh):
    placed = (
        P("group", None, "tensor", None, None),
        P(),
        P(),
        P("group", None, None, "tensor", None),
        P("group", None, None, "tensor", None),
    )
    return jax.shard_map(
        shards,
        mesh=mesh,
        in_specs=placed,
        out_specs=P("group", None, None, "tensor", None),
        check_vma=False,
    )
```

time: 434 us -> 135 us (0.31)
  waiting for transfers between devices: 274 us -> 0 us
  Pallas kernels: 0 us -> 129 us
  starting transfers between devices: 128 us -> 0 us
  local copies, waits for them, and re-layouts: 15.6 us -> 5.67 us
  matrix products: 8.83 us -> 0 us
  other arithmetic: 5.58 us -> 0.1 us
    all_to_all x2 -> x0, waiting for transfers between devices: 274 us -> none  [the longest x1 182 us: shards(): lax.all_to_all(jnp.where(send_live[:, None, None, None, None], chosen, jn...]
    pallas_call x0 -> x1, Pallas kernels: none -> 129 us  [shards(): pl.pallas_call(functools.partial(kernel, groups, tensors), out_shape=jax....]
    all_to_all x2 -> x0, starting transfers between devices: 128 us -> none  [the longest x1 110 us: shards(): lax.all_to_all(jnp.where(send_live[:, None, None, None, None], chosen, jn...]
    dot_general x4 -> x0, matrix products: 8.83 us -> none  [the longest x1 2.91 us: shards(): jnp.einsum('stkgd,spkd->stkgp', queries, ctx_keys, preferred_element_type...]
    gather x2 -> x0, local copies, waits for them, and re-layouts: 5.73 us -> none  [the longest x1 4.93 us: shards(): chosen = jnp.take(by_head, send_index, axis=0)]
    all_to_all x1 -> x0, local copies, waits for them, and re-layouts: 4.77 us -> none  [shards(): lax.all_to_all(cache_blocks, 'tensor', split_axis=3, concat_axis=2, tiled...]
  transfers between devices with their start and end apart: 2 -> 0, of which waited for: 2 -> 0; matrix products, arithmetic and copies ran while one was open for 1% -> 0% of each run, Pallas kernels for 0% -> 0%
where the time goes in v1:
time: 135 us; the launch traced here: 134 us
  Pallas kernels  129 us (96%)
  local copies, waits for them, and re-layouts  5.67 us (4%)
    pallas_call x1, Pallas kernels, shards(): pl.pallas_call(functools.partial(kernel, groups, tensors), out_shape=jax....  129 us
    unnamed x5, local copies, waits for them, and re-layouts  4.02 us

profile of v1, /device:TPU:1, one launch (start us, length us, event | category | flops | bytes accessed | tf_op | source)
XLA Modules:
  0.0 134.5 jit_solution(6138722778882372021)
XLA Ops:
  0.0 0.7 dynamic-slice_bitcast_fusion
  0.7 0.1 select_reduce_fusion
  0.8 0.9 reshape.18.fresh_ref
  1.8 0.0 copy-start
  1.8 2.2 %copy-done = bf16[64,1,16,8,256]{4,3,2,1,0:T(8,128)(2,1)S(1)} copy-done((bf16[64,1,16,8,256]{4,3,2,1,0:T(8,128)(2,1)S(1)}, bf16[64,1,16,8,256]{4,3,2,1,0:T(8,128)(2,1)}, u32[]{:S(2)}) %copy-start) | copy-done | bytes 4194328
  3.9 0.0 copy-start.1
  3.9 1.0 copy-done.1
  5.0 128.7 %shard_map.55 = bf16[64,32,128]{2,1,0:T(8,128)(2,1)S(1)} custom-call(bf16[64,128,256]{2,1,0:T(8,128)(2,1)S(1)} %bitcast.9, s32[64]{0:T(128)S(1)} %get-tuple-element.6.pos_ref, s32[64]{0:T(128)S(1)} %get-tuple-element.5.len_ref, bf16[64,32,128]{2,1,0:T(8,128)(2,1)S(1)} %bitcast.11, bf16[8,32,256]{2,1,0:T(8,128)(2,1)S(1)} %reshape.18.fresh_ref), custom_call_target="tpu_custom_call" | custom-call | flops 1073741824 | bytes 12582912 | tf_op jit(solution)/shard_map/pallas_call | solution.py:252
  133.7 0.8 copy.7
Async XLA Ops:
  1.8 2.2 %copy-start = (bf16[64,1,16,8,256]{4,3,2,1,0:T(8,128)(2,1)S(1)}, bf16[64,1,16,8,256]{4,3,2,1,0:T(8,128)(2,1)}, u32[]{:S(2)}) copy-start(bf16[64,1,16,8,256]{4,3,2,1,0:T(8,128)(2,1)} %param.5) | copy-start | bytes 12582916
  3.9 1.0 copy-start.1

commit v2 on v1

v2 whole, which is shorter than its diff:
```python
import functools
import math

import jax
import jax.numpy as jnp
from jax import lax
from jax.experimental import pallas as pl
from jax.experimental.pallas import tpu as pltpu
from jax.sharding import PartitionSpec as P

MESH = pl.DeviceIdType.MESH

X, ZL, CORES = 4, 8, 2
ZH = 2
CHUNKS = 8
NONE = -1e30


def kernel(groups, tensors, cache_ref, perm_ref, plen_ref, newq_ref, newkv_ref, out_ref,
           cbuf, q_ref, fresh_ref, perm_v, plen_v, meta, where_ref, kvsend, kvrecv, qbuf, osend, orecv, ssend, srecv, fo, fm, fl,
           cache_sem, in_sem, meet_sem, kv_send_sem, kv_recv_sem, q_send_sem, q_recv_sem,
           o_send_sem, o_recv_sem, s_send_sem, s_recv_sem):
    ys = tensors // ZH
    zs = ZH * ZL
    plane = X * CORES
    g = lax.axis_index("group")
    t = lax.axis_index("tensor")
    y, zh = t // ZH, t % ZH
    core, zl, x = g % CORES, (g // CORES) % ZL, g // (CORES * ZL)
    z = zh * ZL + zl
    rows, qn, head = q_ref.shape
    steps = fresh_ref.shape[1]
    tok = cache_ref.shape[1] // tensors
    piece = ZH * tok
    per = rows // CHUNKS
    scale = 1.0 / math.sqrt(head)
    last = groups - 1

    def group_of(px, pz, pc):
        return (px * ZL + pz % ZL) * CORES + pc

    def tensor_of(pz):
        return y * ZH + pz // ZL

    def ahead(dx, dz, dc):
        return (x + dx) % X, (z + dz) % zs, (core + dc) % CORES

    def q_target(i):
        k, j = i // plane, plane - 1 - i % plane
        far = (zs // 2 + (1 - 2 * (k % 2)) * ((k + 1) // 2)) % zs
        return ahead(j // CORES, far, j % CORES)

    def step_offset(i):
        j = plane - 1 - i // ZL
        k = (i + j) % ZL
        far = ZL // 2 + (k // 2) * (1 - k % 2) - ((k + 1) // 2) * (k % 2)
        return j // CORES, far, j % CORES

    def towards(i):
        dx, dz, dc = step_offset(i)
        return (((x + dx) % X) * ZL + (zl + dz) % ZL) * CORES + (core + dc) % CORES

    def source(i):
        dx, dz, dc = step_offset(i)
        return (((x + X - dx) % X) * ZL + (zl + ZL - dz) % ZL) * CORES + (core + CORES - dc) % CORES

    def cache_copy(c):
        return pltpu.make_async_copy(
            cache_ref.at[pl.ds(c * per, per)], cbuf.at[pl.ds(c * per, per)], cache_sem.at[c])

    staged = [
        pltpu.make_async_copy(src, dst, in_sem.at[n])
        for n, (src, dst) in enumerate(
            ((newq_ref, q_ref), (newkv_ref, fresh_ref), (perm_ref, perm_v), (plen_ref, plen_v)))
    ]
    cache_copy(0).start()
    staged[0].start()
    for c in range(1, CHUNKS):
        cache_copy(c).start()
    for copy in staged[1:]:
        copy.start()

    barrier = pltpu.get_barrier_semaphore()

    def greet(sem, px, pz, pc):
        pl.semaphore_signal(
            sem, inc=1, device_id=(group_of(px, pz, pc), tensor_of(pz)), device_id_type=MESH)

    for k in range(1, ys):
        pl.semaphore_signal(barrier, inc=1, device_id=(g, ((y + k) % ys) * ZH + zh), device_id_type=MESH)
    for dz in range(1, zs):
        greet(barrier, *ahead(0, dz, 0))
    for j in range(1, plane):
        greet(barrier, *ahead(j // CORES, 0, j % CORES))

    size = tensors * tok
    r_out = lax.broadcasted_iota(jnp.int32, (size, size), 0)
    r_in = lax.broadcasted_iota(jnp.int32, (size, size), 1)
    pair = r_out // piece + y
    pair = jnp.where(pair >= ys, pair - ys, pair)
    wanted = (r_out % tok) * tensors + pair * ZH + (r_out % piece) // tok
    shuffle = jnp.where(wanted == r_in, 1.0, 0.0).astype(jnp.bfloat16)

    def kv_copy(k, c):
        return pltpu.make_async_remote_copy(
            src_ref=kvsend.at[k - 1, pl.ds(c * per, per)],
            dst_ref=kvrecv.at[pl.ds(c * per, per), y],
            send_sem=kv_send_sem.at[k - 1, c], recv_sem=kv_recv_sem.at[k - 1, c],
            device_id=(g, ((y + k) % ys) * ZH + zh), device_id_type=MESH)

    def regroup(c):
        cache_copy(c).wait()

        def one(i, _):
            for u in range(2):
                r = c * per + i * 2 + u
                moved = jnp.dot(shuffle, cbuf[r], preferred_element_type=jnp.float32).astype(jnp.bfloat16)
                kvrecv[r, y] = moved[:piece]
                for k in range(1, ys):
                    kvsend[k - 1, r] = moved[k * piece:(k + 1) * piece]
            return 0

        lax.fori_loop(0, per // 2, one, 0)

    def send_kv(c):
        for k in range(1, ys):
            kv_copy(k, c).start()

    def q_copy(peer, tensor):
        return pltpu.make_async_remote_copy(
            src_ref=q_ref.at[peer], dst_ref=qbuf.at[g, zh], send_sem=q_send_sem,
            recv_sem=q_recv_sem.at[g], device_id=(peer, tensor), device_id_type=MESH)

    def send_q(i, _):
        px, pz, pc = q_target(i)
        q_copy(group_of(px, pz, pc), tensor_of(pz)).start()
        return 0

    regroup(0)
    pl.semaphore_wait(barrier, ys - 1 + zs - 1 + plane - 1)
    for j in range(1, plane):
        greet(meet_sem, *ahead(j // CORES, 0, j % CORES))
    send_kv(0)
    staged[0].wait()
    regroup(1)
    send_kv(1)
    pl.semaphore_wait(meet_sem, plane - 1)
    pltpu.make_async_copy(q_ref.at[g], qbuf.at[g, zh], q_recv_sem.at[g]).start()
    queries = zs * plane - 1
    share = -(-queries // max(CHUNKS - 2, 1))
    done = 0
    for c in range(2, CHUNKS):
        lax.fori_loop(done, min(done + share, queries), send_q, 0)
        done = min(done + share, queries)
        regroup(c)
        send_kv(c)
    lax.fori_loop(done, queries, send_q, 0)

    staged[2].wait()
    staged[3].wait()
    square = (groups, rows)
    down = lax.broadcasted_iota(jnp.int32, square, 0)
    along = lax.broadcasted_iota(jnp.int32, square, 1)

    def column(ref):
        row = jnp.broadcast_to(ref[pl.ds(g, 1), :], square)
        return jnp.sum(jnp.where(down == along, row, 0), axis=1, keepdims=True)

    match = column(perm_v) == along
    position = jnp.sum(jnp.where(match, down, 0), axis=0, keepdims=True)
    length = jnp.sum(jnp.where(match, column(plen_v), 0), axis=0, keepdims=True)
    meta[0:1, 0:groups] = jnp.minimum(position, rows - 1)
    meta[1:2, 0:groups] = jnp.where(position < rows, length, 0)
    to_scalar = pltpu.make_async_copy(meta, where_ref, in_sem.at[2])
    to_scalar.start()

    staged[1].wait()
    at = per
    shape = (at, qn, steps)
    f_keep = lax.broadcasted_iota(jnp.int32, shape, 2) <= lax.broadcasted_iota(jnp.int32, shape, 1) // (qn // steps)

    def fresh_part(b, _):
        q = q_ref[pl.ds(b * at, at)]
        kv = fresh_ref[pl.ds(b * at, at)]
        s = jnp.einsum("bqd,bud->bqu", q, kv[:, :, :head], preferred_element_type=jnp.float32) * scale
        s = jnp.where(f_keep, s, NONE)
        m = jnp.max(s, axis=2, keepdims=True)
        p = jnp.exp(s - m)
        l = jnp.sum(p, axis=2, keepdims=True)
        o = jnp.einsum("bqu,bud->bqd", p.astype(jnp.bfloat16), kv[:, :, head:], preferred_element_type=jnp.float32)
        fo[pl.ds(b * at, at)] = o
        fm[pl.ds(b * at, at)] = jnp.broadcast_to(m, (at, qn, head))
        fl[pl.ds(b * at, at)] = jnp.broadcast_to(l, (at, qn, head))
        return 0

    lax.fori_loop(0, rows // at, fresh_part, 0)
    to_scalar.wait()

    for c in range(CHUNKS):
        for k in range(1, ys):
            kv_copy(k, c).wait_recv()

    both = ZH * qn
    shape = (both, ys * piece)
    a_row = lax.broadcasted_iota(jnp.int32, shape, 0)
    a_col = lax.broadcasted_iota(jnp.int32, shape, 1)
    token = ((a_col // piece) * ZH + zh) * tok + a_col % tok
    token = jnp.where((a_col % piece) // tok == a_row // qn, token, 1 << 20)
    lane = lax.broadcasted_iota(jnp.int32, (both, head), 1)
    diag = lax.broadcasted_iota(jnp.int32, (both, head), 0) % qn
    on_m, on_l = lane == diag, lane == diag + qn

    def o_copy(peer, h):
        return pltpu.make_async_remote_copy(
            src_ref=osend.at[peer, h], dst_ref=orecv.at[g, zh], send_sem=o_send_sem,
            recv_sem=o_recv_sem.at[g], device_id=(peer, y * ZH + h), device_id_type=MESH)

    def s_copy(peer, h):
        return pltpu.make_async_remote_copy(
            src_ref=ssend.at[peer, h], dst_ref=srecv.at[g, zh], send_sem=s_send_sem,
            recv_sem=s_recv_sem.at[g], device_id=(peer, y * ZH + h), device_id_type=MESH)

    def attend(i):
        src = source(i)
        pltpu.make_async_copy(qbuf.at[src], qbuf.at[src], q_recv_sem.at[src]).wait()
        q = qbuf[src].reshape(both, head)
        kv = kvrecv[where_ref[0, src]].reshape(ys * piece, 2 * head)
        s = lax.dot_general(q, kv[:, :head], (((1,), (1,)), ((), ())), preferred_element_type=jnp.float32) * scale
        keep = token < where_ref[1, src]
        s = jnp.where(keep, s, NONE)
        m = jnp.max(s, axis=1, keepdims=True)
        p = jnp.where(keep, jnp.exp(s - m), 0.0)
        l = jnp.sum(p, axis=1, keepdims=True)
        o = jnp.dot(p.astype(jnp.bfloat16), kv[:, head:], preferred_element_type=jnp.float32)
        osend[src] = o.astype(jnp.bfloat16).reshape(ZH, qn, head)
        stat = jnp.where(on_m, m, jnp.where(on_l, l, 0.0))
        ssend[src] = jnp.sum(stat.reshape(ZH, qn, head), axis=1, keepdims=True)
        return src

    def attend_send(i, _):
        src = attend(i)
        for h in range(ZH):
            s_copy(src, h).start()
            o_copy(src, h).start()
        return 0

    lax.fori_loop(0, last, attend_send, 0)
    attend(last)
    s_copy(g, 1 - zh).start()
    o_copy(g, 1 - zh).start()
    pltpu.make_async_copy(osend.at[g, zh], orecv.at[g, zh], o_recv_sem.at[g]).start()
    pltpu.make_async_copy(ssend.at[g, zh], srecv.at[g, zh], s_recv_sem.at[g]).start()

    c_lane = lax.broadcasted_iota(jnp.int32, (qn, head), 1)
    c_row = lax.broadcasted_iota(jnp.int32, (qn, head), 0)

    def combine(i, _):
        src = towards(i)
        pltpu.make_async_copy(srecv.at[src], srecv.at[src], s_recv_sem.at[src]).wait()
        pltpu.make_async_copy(orecv.at[src], orecv.at[src], o_recv_sem.at[src]).wait()
        m, l, o = [fm[src]], [fl[src]], [fo[src]]
        for h in range(ZH):
            stat = jnp.broadcast_to(srecv[src, h], (qn, head))
            m.append(jnp.sum(jnp.where(c_lane == c_row, stat, 0.0), axis=1, keepdims=True))
            l.append(jnp.sum(jnp.where(c_lane == c_row + qn, stat, 0.0), axis=1, keepdims=True))
            o.append(orecv[src, h].astype(jnp.float32))
        top = functools.reduce(jnp.maximum, m)
        w = [jnp.exp(a - top) for a in m]
        den = sum(a * b for a, b in zip(w, l))
        num = sum(a * b for a, b in zip(w, o))
        out_ref[src] = (num / den).astype(jnp.bfloat16)
        return 0

    lax.fori_loop(0, groups, combine, 0)

    for c in range(CHUNKS):
        for k in range(1, ys):
            kv_copy(k, c).wait_send()
    for ref, sem in ((qbuf, q_send_sem), (osend, o_send_sem), (ssend, s_send_sem)):
        pltpu.make_async_copy(ref.at[pl.ds(0, last)], ref.at[pl.ds(0, last)], sem).wait()
        pltpu.make_async_copy(ref.at[last, 0], ref.at[last, 0], sem).wait()


def shards(cache_blocks, prompt_len, dest_perm, new_q, new_kv):
    groups = lax.axis_size("group")
    tensors = lax.axis_size("tensor")
    requests, _, tok, heads, width = cache_blocks.shape
    head = width // 2
    slots, steps, q_here = new_q.shape[1:4]
    qn = steps * q_here
    cache = cache_blocks.reshape(requests, tok * heads, width)
    queries = new_q.reshape(slots, qn, head)
    fresh = new_kv.reshape(slots, steps, width)
    ys = tensors // ZH
    piece = ZH * tok
    bf16, f32, i32 = jnp.bfloat16, jnp.float32, jnp.int32
    anywhere = pl.BlockSpec(memory_space=pl.ANY)
    dma = pltpu.SemaphoreType.DMA
    out = pl.pallas_call(
        functools.partial(kernel, groups, tensors),
        out_shape=jax.ShapeDtypeStruct((slots, qn, head), bf16),
        in_specs=[anywhere] * 5,
        out_specs=pl.BlockSpec(memory_space=pltpu.VMEM),
        scratch_shapes=[
            pltpu.VMEM((requests, tok * heads, width), bf16),
            pltpu.VMEM((slots, qn, head), bf16),
            pltpu.VMEM((slots, steps, width), bf16),
            pltpu.VMEM(dest_perm.shape, i32),
            pltpu.VMEM(prompt_len.shape, i32),
            pltpu.VMEM((8, 128), i32),
            pltpu.SMEM((8, 128), i32),
            pltpu.VMEM((ys - 1, requests, piece, width), bf16),
            pltpu.VMEM((requests, ys, piece, width), bf16),
            pltpu.VMEM((groups, ZH, qn, head), bf16),
            pltpu.VMEM((groups, ZH, qn, head), bf16),
            pltpu.VMEM((groups, ZH, qn, head), bf16),
            pltpu.VMEM((groups, ZH, 1, head), f32),
            pltpu.VMEM((groups, ZH, 1, head), f32),
            pltpu.VMEM((slots, qn, head), f32),
            pltpu.VMEM((slots, qn, head), f32),
            pltpu.VMEM((slots, qn, head), f32),
            dma((CHUNKS,)),
            dma((4,)),
            pltpu.SemaphoreType.REGULAR,
            dma((ys - 1, CHUNKS)),
            dma((ys - 1, CHUNKS)),
            dma,
            dma((groups,)),
            dma,
            dma((groups,)),
            dma,
            dma((groups,)),
        ],
        compiler_params=pltpu.CompilerParams(
            collective_id=0, has_side_effects=True, vmem_limit_bytes=58 << 20),
        cost_estimate=pl.CostEstimate(flops=1 << 30, bytes_accessed=12 << 20, transcendentals=1 << 20),
    )(cache, dest_perm, prompt_len, queries, fresh)
    return out.reshape(1, slots, steps, q_here, head)


def solution(mesh):
    placed = (
        P("group", None, "tensor", None, None),
        P(),
        P(),
        P("group", None, None, "tensor", None),
        P("group", None, None, "tensor", None),
    )
    return jax.shard_map(
        shards,
        mesh=mesh,
        in_specs=placed,
        out_specs=P("group", None, None, "tensor", None),
        check_vma=False,
    )
```

time: 135 us -> 121 us (0.90)
  Pallas kernels: 129 us -> 119 us
  local copies, waits for them, and re-layouts: 5.67 us -> 1.87 us
    pallas_call x1, Pallas kernels: 129 us -> 119 us  [shards(): pl.pallas_call(functools.partial(kernel, groups, tensors), out_shape=jax....]
    unnamed x5 -> x1, local copies, waits for them, and re-layouts: 4.02 us -> 1.87 us
where the time goes in v2:
time: 121 us; the launch traced here: 120 us
  Pallas kernels  119 us (98%)
  local copies, waits for them, and re-layouts  1.87 us (2%)
    pallas_call x1, Pallas kernels, shards(): pl.pallas_call(functools.partial(kernel, groups, tensors), out_shape=jax....  119 us

profile of v2, /device:TPU:1, one launch (start us, length us, event | category | flops | bytes accessed | tf_op | source)
XLA Modules:
  0.0 120.4 jit_solution(8448702745122116477)
XLA Ops:
  0.0 118.5 %shard_map.55 = bf16[64,32,128]{2,1,0:T(8,128)(2,1)} custom-call(bf16[64,128,256]{2,1,0:T(8,128)(2,1)} %bitcast.4, s32[64,64]{1,0:T(8,128)} %perm_ref.1, s32[64,64]{1,0:T(8,128)} %plen_ref.1, bf16[64,32,128]{2,1,0:T(8,128)(2,1)} %bitcast.6, bf16[64,4,256]{2,1,0:T(4,128)(2,1)} %bitcast.7), custom_call_target="tpu_custom_call" | custom-call | flops 1073741824 | bytes 12582912 | tf_op jit(solution)/shard_map/pallas_call | solution.py:299
  118.5 1.9 %copy.7 = bf16[1,64,4,8,128]{4,3,2,1,0:T(8,128)(2,1)} copy(bf16[1,64,4,8,128]{4,3,2,1,0:T(8,128)(2,1)} %bitcast.5) | data formatting | bytes 1048576

commit v3 on v2

--- a/solution.py
+++ b/solution.py
@@ -45,14 +45,10 @@
     def ahead(dx, dz, dc):
         return (x + dx) % X, (z + dz) % zs, (core + dc) % CORES
 
-    def q_target(i):
-        k, j = i // plane, plane - 1 - i % plane
-        far = (zs // 2 + (1 - 2 * (k % 2)) * ((k + 1) // 2)) % zs
-        return ahead(j // CORES, far, j % CORES)
-
     def step_offset(i):
-        j = plane - 1 - i // ZL
-        k = (i + j) % ZL
+        n = (i + 1) % groups
+        j = n // ZL
+        k = ZL - 1 - (n + j) % ZL
         far = ZL // 2 + (k // 2) * (1 - k % 2) - ((k + 1) // 2) * (k % 2)
         return j // CORES, far, j % CORES
 
@@ -73,11 +69,11 @@
         for n, (src, dst) in enumerate(
             ((newq_ref, q_ref), (newkv_ref, fresh_ref), (perm_ref, perm_v), (plen_ref, plen_v)))
     ]
-    cache_copy(0).start()
-    staged[0].start()
-    for c in range(1, CHUNKS):
+    for copy in staged[2:]:
+        copy.start()
+    for c in range(CHUNKS):
         cache_copy(c).start()
-    for copy in staged[1:]:
+    for copy in staged[:2]:
         copy.start()
 
     barrier = pltpu.get_barrier_semaphore()
@@ -92,6 +88,24 @@
         greet(barrier, *ahead(0, dz, 0))
     for j in range(1, plane):
         greet(barrier, *ahead(j // CORES, 0, j % CORES))
+
+    staged[2].wait()
+    staged[3].wait()
+    square = (groups, rows)
+    down = lax.broadcasted_iota(jnp.int32, square, 0)
+    along = lax.broadcasted_iota(jnp.int32, square, 1)
+
+    def column(ref):
+        row = jnp.broadcast_to(ref[pl.ds(g, 1), :], square)
+        return jnp.sum(jnp.where(down == along, row, 0), axis=1, keepdims=True)
+
+    match = column(perm_v) == along
+    position = jnp.sum(jnp.where(match, down, 0), axis=0, keepdims=True)
+    length = jnp.sum(jnp.where(match, column(plen_v), 0), axis=0, keepdims=True)
+    meta[0:1, 0:groups] = jnp.minimum(position, rows - 1)
+    meta[1:2, 0:groups] = jnp.where(position < rows, length, 0)
+    to_scalar = pltpu.make_async_copy(meta, where_ref, in_sem.at[2])
+    to_scalar.start()
 
     size = tensors * tok
     r_out = lax.broadcasted_iota(jnp.int32, (size, size), 0)
@@ -109,12 +123,11 @@
             device_id=(g, ((y + k) % ys) * ZH + zh), device_id_type=MESH)
 
     def regroup(c):
-        cache_copy(c).wait()
-
         def one(i, _):
             for u in range(2):
                 r = c * per + i * 2 + u
-                moved = jnp.dot(shuffle, cbuf[r], preferred_element_type=jnp.float32).astype(jnp.bfloat16)
+                cache = cbuf[where_ref[0, source(r)]]
+                moved = jnp.dot(shuffle, cache, preferred_element_type=jnp.float32).astype(jnp.bfloat16)
                 kvrecv[r, y] = moved[:piece]
                 for k in range(1, ys):
                     kvsend[k - 1, r] = moved[k * piece:(k + 1) * piece]
@@ -132,47 +145,35 @@
             recv_sem=q_recv_sem.at[g], device_id=(peer, tensor), device_id_type=MESH)
 
     def send_q(i, _):
-        px, pz, pc = q_target(i)
-        q_copy(group_of(px, pz, pc), tensor_of(pz)).start()
+        peer = towards(i)
+        for h in range(ZH):
+            q_copy(peer, y * ZH + h).start()
         return 0
 
+    to_scalar.wait()
+    for c in range(CHUNKS):
+        cache_copy(c).wait()
     regroup(0)
+    staged[0].wait()
+    pltpu.make_async_copy(q_ref.at[g], qbuf.at[g, zh], q_recv_sem.at[g]).start()
     pl.semaphore_wait(barrier, ys - 1 + zs - 1 + plane - 1)
     for j in range(1, plane):
         greet(meet_sem, *ahead(j // CORES, 0, j % CORES))
+    line = ZL - 1
+    lax.fori_loop(0, line, send_q, 0)
+    q_copy(g, y * ZH + 1 - zh).start()
     send_kv(0)
-    staged[0].wait()
     regroup(1)
     send_kv(1)
     pl.semaphore_wait(meet_sem, plane - 1)
-    pltpu.make_async_copy(q_ref.at[g], qbuf.at[g, zh], q_recv_sem.at[g]).start()
-    queries = zs * plane - 1
-    share = -(-queries // max(CHUNKS - 2, 1))
-    done = 0
+    done = line
     for c in range(2, CHUNKS):
-        lax.fori_loop(done, min(done + share, queries), send_q, 0)
-        done = min(done + share, queries)
+        upto = line + (last - line) * (c - 1) // (CHUNKS - 2)
+        lax.fori_loop(done, upto, send_q, 0)
+        done = upto
         regroup(c)
         send_kv(c)
-    lax.fori_loop(done, queries, send_q, 0)
-
-    staged[2].wait()
-    staged[3].wait()
-    square = (groups, rows)
-    down = lax.broadcasted_iota(jnp.int32, square, 0)
-    along = lax.broadcasted_iota(jnp.int32, square, 1)
-
-    def column(ref):
-        row = jnp.broadcast_to(ref[pl.ds(g, 1), :], square)
-        return jnp.sum(jnp.where(down == along, row, 0), axis=1, keepdims=True)
-
-    match = column(perm_v) == along
-    position = jnp.sum(jnp.where(match, down, 0), axis=0, keepdims=True)
-    length = jnp.sum(jnp.where(match, column(plen_v), 0), axis=0, keepdims=True)
-    meta[0:1, 0:groups] = jnp.minimum(position, rows - 1)
-    meta[1:2, 0:groups] = jnp.where(position < rows, length, 0)
-    to_scalar = pltpu.make_async_copy(meta, where_ref, in_sem.at[2])
-    to_scalar.start()
+    lax.fori_loop(done, last, send_q, 0)
 
     staged[1].wait()
     at = per
@@ -194,11 +195,6 @@
         return 0
 
     lax.fori_loop(0, rows // at, fresh_part, 0)
-    to_scalar.wait()
-
-    for c in range(CHUNKS):
-        for k in range(1, ys):
-            kv_copy(k, c).wait_recv()
 
     both = ZH * qn
     shape = (both, ys * piece)
@@ -224,7 +220,7 @@
         src = source(i)
         pltpu.make_async_copy(qbuf.at[src], qbuf.at[src], q_recv_sem.at[src]).wait()
         q = qbuf[src].reshape(both, head)
-        kv = kvrecv[where_ref[0, src]].reshape(ys * piece, 2 * head)
+        kv = kvrecv[i].reshape(ys * piece, 2 * head)
         s = lax.dot_general(q, kv[:, :head], (((1,), (1,)), ((), ())), preferred_element_type=jnp.float32) * scale
         keep = token < where_ref[1, src]
         s = jnp.where(keep, s, NONE)
@@ -244,7 +240,10 @@
             o_copy(src, h).start()
         return 0
 
-    lax.fori_loop(0, last, attend_send, 0)
+    for c in range(CHUNKS):
+        for k in range(1, ys):
+            kv_copy(k, c).wait_recv()
+        lax.fori_loop(c * per, min((c + 1) * per, last), attend_send, 0)
     attend(last)
     s_copy(g, 1 - zh).start()
     o_copy(g, 1 - zh).start()
@@ -294,12 +293,12 @@
     ys = tensors // ZH
     piece = ZH * tok
     bf16, f32, i32 = jnp.bfloat16, jnp.float32, jnp.int32
-    anywhere = pl.BlockSpec(memory_space=pl.ANY)
+    hbm = pl.BlockSpec(memory_space=pltpu.HBM)
     dma = pltpu.SemaphoreType.DMA
     out = pl.pallas_call(
         functools.partial(kernel, groups, tensors),
         out_shape=jax.ShapeDtypeStruct((slots, qn, head), bf16),
-        in_specs=[anywhere] * 5,
+        in_specs=[hbm] * 5,
         out_specs=pl.BlockSpec(memory_space=pltpu.VMEM),
         scratch_shapes=[
             pltpu.VMEM((requests, tok * heads, width), bf16),
@@ -332,9 +331,9 @@
             dma((groups,)),
         ],
         compiler_params=pltpu.CompilerParams(
-            collective_id=0, has_side_effects=True, vmem_limit_bytes=58 << 20),
+            collective_id=0, has_side_effects=True, vmem_limit_bytes=48 << 20),
         cost_estimate=pl.CostEstimate(flops=1 << 30, bytes_accessed=12 << 20, transcendentals=1 << 20),
-    )(cache, dest_perm, prompt_len, queries, fresh)
+    )(*(pltpu.with_memory_space_constraint(a, pltpu.HBM) for a in (cache, dest_perm, prompt_len, queries, fresh)))
     return out.reshape(1, slots, steps, q_here, head)
 
 

time: 121 us -> 115 us (0.950)
  Pallas kernels: 119 us -> 114 us
    pallas_call x1, Pallas kernels: 119 us -> 114 us  [shards(): pl.pallas_call(functools.partial(kernel, groups, tensors), out_shape=jax....]
where the time goes in v3:
time: 115 us
  Pallas kernels  114 us (99%)
    pallas_call x1, Pallas kernels, shards(): pl.pallas_call(functools.partial(kernel, groups, tensors), out_shape=jax....  114 us

profile of v3, /device:TPU:1, one launch (start us, length us, event | category | flops | bytes accessed | tf_op | source)
XLA Modules:
  0.0 115.2 jit_solution(17605876718916209146)
XLA Ops:
  0.0 114.4 %shard_map.55 = bf16[64,32,128]{2,1,0:T(8,128)(2,1)S(1)} custom-call(bf16[64,128,256]{2,1,0:T(8,128)(2,1)} %bitcast.5, s32[64,64]{1,0:T(8,128)} %perm_ref.1, s32[64,64]{1,0:T(8,128)} %plen_ref.1, bf16[64,32,128]{2,1,0:T(8,128)(2,1)} %bitcast.6, bf16[64,4,256]{2,1,0:T(4,128)(2,1)} %bitcast.7), custom_call_target="tpu_custom_call" | custom-call | flops 1073741824 | bytes 12582912 | tf_op jit(solution)/shard_map/pallas_call | solution.py:298
  114.4 0.8 copy.7

commit v4 on v3

--- a/solution.py
+++ b/solution.py
@@ -46,10 +46,12 @@
         return (x + dx) % X, (z + dz) % zs, (core + dc) % CORES
 
     def step_offset(i):
-        n = (i + 1) % groups
-        j = n // ZL
-        k = ZL - 1 - (n + j) % ZL
-        far = ZL // 2 + (k // 2) * (1 - k % 2) - ((k + 1) // 2) * (k % 2)
+        n = i - (ZL - 1)
+        later = (n + groups) // groups
+        rest = later * (1 - (i + 1) // groups)
+        j = rest * (n * later % (plane - 1) + 1)
+        k = (1 - later) * (i + 1) + rest * (n * later // (plane - 1))
+        far = (k % 2) * (ZL - 1 - k // 2) + (1 - k % 2) * (k // 2)
         return j // CORES, far, j % CORES
 
     def towards(i):
@@ -202,8 +204,8 @@
     a_col = lax.broadcasted_iota(jnp.int32, shape, 1)
     token = ((a_col // piece) * ZH + zh) * tok + a_col % tok
     token = jnp.where((a_col % piece) // tok == a_row // qn, token, 1 << 20)
-    lane = lax.broadcasted_iota(jnp.int32, (both, head), 1)
-    diag = lax.broadcasted_iota(jnp.int32, (both, head), 0) % qn
+    lane = lax.broadcasted_iota(jnp.int32, (both, 2 * qn), 1)
+    diag = lax.broadcasted_iota(jnp.int32, (both, 2 * qn), 0) % qn
     on_m, on_l = lane == diag, lane == diag + qn
 
     def o_copy(peer, h):
@@ -230,7 +232,7 @@
         o = jnp.dot(p.astype(jnp.bfloat16), kv[:, head:], preferred_element_type=jnp.float32)
         osend[src] = o.astype(jnp.bfloat16).reshape(ZH, qn, head)
         stat = jnp.where(on_m, m, jnp.where(on_l, l, 0.0))
-        ssend[src] = jnp.sum(stat.reshape(ZH, qn, head), axis=1, keepdims=True)
+        ssend[src] = jnp.sum(stat.reshape(ZH, qn, 2 * qn), axis=1, keepdims=True)
         return src
 
     def attend_send(i, _):
@@ -250,8 +252,8 @@
     pltpu.make_async_copy(osend.at[g, zh], orecv.at[g, zh], o_recv_sem.at[g]).start()
     pltpu.make_async_copy(ssend.at[g, zh], srecv.at[g, zh], s_recv_sem.at[g]).start()
 
-    c_lane = lax.broadcasted_iota(jnp.int32, (qn, head), 1)
-    c_row = lax.broadcasted_iota(jnp.int32, (qn, head), 0)
+    c_lane = lax.broadcasted_iota(jnp.int32, (qn, 2 * qn), 1)
+    c_row = lax.broadcasted_iota(jnp.int32, (qn, 2 * qn), 0)
 
     def combine(i, _):
         src = towards(i)
@@ -259,7 +261,7 @@
         pltpu.make_async_copy(orecv.at[src], orecv.at[src], o_recv_sem.at[src]).wait()
         m, l, o = [fm[src]], [fl[src]], [fo[src]]
         for h in range(ZH):
-            stat = jnp.broadcast_to(srecv[src, h], (qn, head))
+            stat = jnp.broadcast_to(srecv[src, h], (qn, 2 * qn))
             m.append(jnp.sum(jnp.where(c_lane == c_row, stat, 0.0), axis=1, keepdims=True))
             l.append(jnp.sum(jnp.where(c_lane == c_row + qn, stat, 0.0), axis=1, keepdims=True))
             o.append(orecv[src, h].astype(jnp.float32))
@@ -313,8 +315,8 @@
             pltpu.VMEM((groups, ZH, qn, head), bf16),
             pltpu.VMEM((groups, ZH, qn, head), bf16),
             pltpu.VMEM((groups, ZH, qn, head), bf16),
-            pltpu.VMEM((groups, ZH, 1, head), f32),
-            pltpu.VMEM((groups, ZH, 1, head), f32),
+            pltpu.VMEM((groups, ZH, 1, 2 * qn), f32),
+            pltpu.VMEM((groups, ZH, 1, 2 * qn), f32),
             pltpu.VMEM((slots, qn, head), f32),
             pltpu.VMEM((slots, qn, head), f32),
             pltpu.VMEM((slots, qn, head), f32),

time: 115 us -> 115 us (level)
  no operation moved by 1% of the time
where the time goes in v4:
time: 115 us
  Pallas kernels  115 us (100%)
    pallas_call x1, Pallas kernels, shards(): pl.pallas_call(functools.partial(kernel, groups, tensors), out_shape=jax....  115 us

profile of v4, /device:TPU:1, one launch (start us, length us, event | category | flops | bytes accessed | tf_op | source)
XLA Modules:
  0.0 115.4 jit_solution(1587681444353417445)
XLA Ops:
  0.0 114.6 %shard_map.55 = bf16[64,32,128]{2,1,0:T(8,128)(2,1)S(1)} custom-call(bf16[64,128,256]{2,1,0:T(8,128)(2,1)} %bitcast.5, s32[64,64]{1,0:T(8,128)} %perm_ref.1, s32[64,64]{1,0:T(8,128)} %plen_ref.1, bf16[64,32,128]{2,1,0:T(8,128)(2,1)} %bitcast.6, bf16[64,4,256]{2,1,0:T(4,128)(2,1)} %bitcast.7), custom_call_target="tpu_custom_call" | custom-call | flops 1073741824 | bytes 12582912 | tf_op jit(solution)/shard_map/pallas_call | solution.py:300
  114.6 0.8 copy.7

commit v5 on v4

--- a/solution.py
+++ b/solution.py
@@ -13,6 +13,7 @@
 X, ZL, CORES = 4, 8, 2
 ZH = 2
 CHUNKS = 8
+BEHIND = 3
 NONE = -1e30
 
 
@@ -46,12 +47,10 @@
         return (x + dx) % X, (z + dz) % zs, (core + dc) % CORES
 
     def step_offset(i):
-        n = i - (ZL - 1)
-        later = (n + groups) // groups
-        rest = later * (1 - (i + 1) // groups)
-        j = rest * (n * later % (plane - 1) + 1)
-        k = (1 - later) * (i + 1) + rest * (n * later // (plane - 1))
-        far = (k % 2) * (ZL - 1 - k // 2) + (1 - k % 2) * (k // 2)
+        n = (i + 1) % groups
+        j = n // ZL
+        k = ZL - 1 - (n + j) % ZL
+        far = ZL // 2 + (k // 2) * (1 - k % 2) - ((k + 1) // 2) * (k % 2)
         return j // CORES, far, j % CORES
 
     def towards(i):
@@ -71,12 +70,11 @@
         for n, (src, dst) in enumerate(
             ((newq_ref, q_ref), (newkv_ref, fresh_ref), (perm_ref, perm_v), (plen_ref, plen_v)))
     ]
-    for copy in staged[2:]:
+    for copy in staged[2:] + staged[:1]:
         copy.start()
     for c in range(CHUNKS):
         cache_copy(c).start()
-    for copy in staged[:2]:
-        copy.start()
+    staged[1].start()
 
     barrier = pltpu.get_barrier_semaphore()
 
@@ -152,10 +150,6 @@
             q_copy(peer, y * ZH + h).start()
         return 0
 
-    to_scalar.wait()
-    for c in range(CHUNKS):
-        cache_copy(c).wait()
-    regroup(0)
     staged[0].wait()
     pltpu.make_async_copy(q_ref.at[g], qbuf.at[g, zh], q_recv_sem.at[g]).start()
     pl.semaphore_wait(barrier, ys - 1 + zs - 1 + plane - 1)
@@ -164,9 +158,12 @@
     line = ZL - 1
     lax.fori_loop(0, line, send_q, 0)
     q_copy(g, y * ZH + 1 - zh).start()
-    send_kv(0)
-    regroup(1)
-    send_kv(1)
+    to_scalar.wait()
+    for c in range(CHUNKS):
+        cache_copy(c).wait()
+    for c in range(2):
+        regroup(c)
+        send_kv(c)
     pl.semaphore_wait(meet_sem, plane - 1)
     done = line
     for c in range(2, CHUNKS):
@@ -242,9 +239,12 @@
             o_copy(src, h).start()
         return 0
 
+    arrived = 0
     for c in range(CHUNKS):
-        for k in range(1, ys):
-            kv_copy(k, c).wait_recv()
+        while arrived < min(c + 1 + BEHIND, CHUNKS):
+            for k in range(1, ys):
+                kv_copy(k, arrived).wait_recv()
+            arrived += 1
         lax.fori_loop(c * per, min((c + 1) * per, last), attend_send, 0)
     attend(last)
     s_copy(g, 1 - zh).start()

time: 115 us -> 116 us (level)
  no operation moved by 1% of the time
where the time goes in v5:
time: 116 us; the launch traced here: 115 us
  Pallas kernels  115 us (99%)
    pallas_call x1, Pallas kernels, shards(): pl.pallas_call(functools.partial(kernel, groups, tensors), out_shape=jax....  115 us

profile of v5, /device:TPU:1, one launch (start us, length us, event | category | flops | bytes accessed | tf_op | source)
XLA Modules:
  0.0 115.5 jit_solution(16390619814133543949)
XLA Ops:
  0.0 114.7 %shard_map.55 = bf16[64,32,128]{2,1,0:T(8,128)(2,1)S(1)} custom-call(bf16[64,128,256]{2,1,0:T(8,128)(2,1)} %bitcast.5, s32[64,64]{1,0:T(8,128)} %perm_ref.1, s32[64,64]{1,0:T(8,128)} %plen_ref.1, bf16[64,32,128]{2,1,0:T(8,128)(2,1)} %bitcast.6, bf16[64,4,256]{2,1,0:T(4,128)(2,1)} %bitcast.7), custom_call_target="tpu_custom_call" | custom-call | flops 1073741824 | bytes 12582912 | tf_op jit(solution)/shard_map/pallas_call | solution.py:300
  114.7 0.8 copy.7

commit v6 on v5

--- a/solution.py
+++ b/solution.py
@@ -154,25 +154,23 @@
     pltpu.make_async_copy(q_ref.at[g], qbuf.at[g, zh], q_recv_sem.at[g]).start()
     pl.semaphore_wait(barrier, ys - 1 + zs - 1 + plane - 1)
     for j in range(1, plane):
-        greet(meet_sem, *ahead(j // CORES, 0, j % CORES))
+        greet(meet_sem.at[j], *ahead(j // CORES, 0, j % CORES))
     line = ZL - 1
     lax.fori_loop(0, line, send_q, 0)
     q_copy(g, y * ZH + 1 - zh).start()
     to_scalar.wait()
     for c in range(CHUNKS):
         cache_copy(c).wait()
-    for c in range(2):
-        regroup(c)
-        send_kv(c)
-    pl.semaphore_wait(meet_sem, plane - 1)
-    done = line
-    for c in range(2, CHUNKS):
-        upto = line + (last - line) * (c - 1) // (CHUNKS - 2)
-        lax.fori_loop(done, upto, send_q, 0)
-        done = upto
-        regroup(c)
-        send_kv(c)
-    lax.fori_loop(done, last, send_q, 0)
+    regroup(0)
+    send_kv(0)
+    for c in range(1, max(CHUNKS, plane)):
+        if c < plane:
+            back = (X - c // CORES) % X * CORES + (CORES - c % CORES) % CORES
+            pl.semaphore_wait(meet_sem.at[back], 1)
+            lax.fori_loop(line + (c - 1) * ZL, line + c * ZL, send_q, 0)
+        if c < CHUNKS:
+            regroup(c)
+            send_kv(c)
 
     staged[1].wait()
     at = per
@@ -322,7 +320,7 @@
             pltpu.VMEM((slots, qn, head), f32),
             dma((CHUNKS,)),
             dma((4,)),
-            pltpu.SemaphoreType.REGULAR,
+            pltpu.SemaphoreType.REGULAR((X * CORES,)),
             dma((ys - 1, CHUNKS)),
             dma((ys - 1, CHUNKS)),
             dma,

time: 116 us -> 116 us (level)
  no operation moved by 1% of the time
where the time goes in v6:
time: 116 us
  Pallas kernels  115 us (99%)
    pallas_call x1, Pallas kernels, shards(): pl.pallas_call(functools.partial(kernel, groups, tensors), out_shape=jax....  115 us

profile of v6, /device:TPU:1, one launch (start us, length us, event | category | flops | bytes accessed | tf_op | source)
XLA Modules:
  0.0 115.9 jit_solution(3797864829526224482)
XLA Ops:
  0.0 115.1 %shard_map.55 = bf16[64,32,128]{2,1,0:T(8,128)(2,1)S(1)} custom-call(bf16[64,128,256]{2,1,0:T(8,128)(2,1)} %bitcast.5, s32[64,64]{1,0:T(8,128)} %perm_ref.1, s32[64,64]{1,0:T(8,128)} %plen_ref.1, bf16[64,32,128]{2,1,0:T(8,128)(2,1)} %bitcast.6, bf16[64,4,256]{2,1,0:T(4,128)(2,1)} %bitcast.7), custom_call_target="tpu_custom_call" | custom-call | flops 1073741824 | bytes 12582912 | tf_op jit(solution)/shard_map/pallas_call | solution.py:298
  115.1 0.8 copy.7

commit v7 on v5

--- a/solution.py
+++ b/solution.py
@@ -147,7 +147,7 @@
     def send_q(i, _):
         peer = towards(i)
         for h in range(ZH):
-            q_copy(peer, y * ZH + h).start()
+            q_copy(peer, y * ZH + (zh + 1 + h) % ZH).start()
         return 0
 
     staged[0].wait()
@@ -235,8 +235,9 @@
     def attend_send(i, _):
         src = attend(i)
         for h in range(ZH):
-            s_copy(src, h).start()
-            o_copy(src, h).start()
+            half = (zh + 1 + h) % ZH
+            s_copy(src, half).start()
+            o_copy(src, half).start()
         return 0
 
     arrived = 0

time: 116 us -> 116 us (level)
  no operation moved by 1% of the time
where the time goes in v7:
time: 116 us; the launch traced here: 115 us
  Pallas kernels  115 us (99%)
    pallas_call x1, Pallas kernels, shards(): pl.pallas_call(functools.partial(kernel, groups, tensors), out_shape=jax....  115 us

profile of v7, /device:TPU:1, one launch (start us, length us, event | category | flops | bytes accessed | tf_op | source)
XLA Modules:
  0.0 115.5 jit_solution(5682899425209341066)
XLA Ops:
  0.0 114.7 %shard_map.55 = bf16[64,32,128]{2,1,0:T(8,128)(2,1)S(1)} custom-call(bf16[64,128,256]{2,1,0:T(8,128)(2,1)} %bitcast.5, s32[64,64]{1,0:T(8,128)} %perm_ref.1, s32[64,64]{1,0:T(8,128)} %plen_ref.1, bf16[64,32,128]{2,1,0:T(8,128)(2,1)} %bitcast.6, bf16[64,4,256]{2,1,0:T(4,128)(2,1)} %bitcast.7), custom_call_target="tpu_custom_call" | custom-call | flops 1073741824 | bytes 12582912 | tf_op jit(solution)/shard_map/pallas_call | solution.py:301
  114.7 0.8 copy.7
